TPU v7x, 32 devices: a whole 2x2x4 slice. The times are simulated.
32 devices in a mesh: wide: 8 (over y, x, core), narrow: 4 (over z).
Axes of the slice: x: 2, y: 2, z: 4, core: 2. Of those that a mesh axis runs over, the one named last changes fastest.
Arguments:
- thinker_rows: bfloat16 [8, 4, 3, 2, 128, 2048], P('wide', 'narrow'), may hold values from -6 to 6
- codec_ids: int32 [8, 4, 3, 2, 128], P('wide', 'narrow'), may hold values from 0 to 2047
- block_lengths: int32 [8, 4, 3, 2], P('wide', 'narrow'), may hold values from 1 to 128
- chosen_label: int32 [8, 4, 3], P('wide', 'narrow'), may hold values from 0 to 1
- ref_logratio: float32 [8, 4, 3], P('wide', 'narrow'), may hold values from -6 to 6
- pair_count: int32 [8, 4], P('wide', 'narrow'), may hold values from 1 to 3, as said below
- proj_weight: bfloat16 [2048, 1024], P('narrow'), may hold values from -0.125 to 0.125
- norm_gain: bfloat16 [1024], P('narrow'), may hold values from 0.25 to 1.75
- head_weight: bfloat16 [1024, 2048], P('narrow')
Outputs:
- loss: float32 [], replicated
- grad_head: float32 [1024, 2048], P('narrow')
- grad_gain: float32 [1024], P('narrow')
Inputs may be any that keep to these rules, and one draw needn't show every extreme that they name: `pair_count`: owners are ordered with the wide index slowest; the counts sum to 64; the sum of the counts of owners below owner i lies between i * 2 and i * 2 + 1; some owner holds 3 live pairs.
All inputs are finite; a program needn't handle non-finite values.
Results may differ from a plain program's by a relative error of at most 0.017.
The roundings to bfloat16 on the way count: a program that leaves them out, or rounds other values in their place, can miss the bound.
Values may be sent and summed in bfloat16 or wider, within the bound.
A program may use at most 64 MiB of HBM per device.

v0:
```python
import jax
import jax.numpy as jnp
from jax import lax
from jax.sharding import PartitionSpec as P

norm_eps = 1e-06
margin_scale = 2.0


def forward_terms(projected, codes, lengths, live_pairs, gain_full, head_full):
    pairs = codes.shape[0]
    frames = codes.shape[2]
    flat = projected.astype(jnp.float32)
    inverse = lax.rsqrt(jnp.mean(flat * flat, axis=1, keepdims=True) + norm_eps)
    normed = (flat * inverse * gain_full.astype(jnp.float32)).astype(jnp.bfloat16)
    logits = jnp.dot(normed, head_full, preferred_element_type=jnp.float32)
    highest = jnp.max(logits, axis=1, keepdims=True)
    log_total = highest + jnp.log(jnp.sum(jnp.exp(logits - highest), axis=1, keepdims=True))
    probs = jnp.exp(logits - log_total)
    target = (lax.broadcasted_iota(jnp.int32, logits.shape, 1) == codes.reshape(-1, 1)).astype(
        jnp.float32
    )
    token_logp = jnp.sum(target * logits, axis=1) - log_total[:, 0]
    frame_index = jnp.arange(frames, dtype=jnp.int32)
    valid = ((frame_index[None, None, :] < lengths[:, :, None]) & live_pairs[:, None, None]).astype(
        jnp.float32
    )
    partial_value = jnp.sum(token_logp.reshape(pairs, 2, frames) * valid, axis=2)
    return (normed, flat, inverse, probs, target, valid, partial_value)


def backward_terms(
    scores, lengths, labels, ratios, live_pairs, flat, inverse, probs, target, valid, head_full
):
    length_f = lengths.astype(jnp.float32)
    score = scores / length_f
    first = labels == 0
    chosen = jnp.where(first, score[:, 0], score[:, 1])
    rejected = jnp.where(first, score[:, 1], score[:, 0])
    margin = margin_scale * (chosen - rejected - ratios)
    live_f = live_pairs.astype(jnp.float32)
    loss_part = jnp.sum(jax.nn.softplus(-margin) * live_f)
    slope = -jax.nn.sigmoid(-margin) * live_f
    weight_first = jnp.where(first, margin_scale * slope, -margin_scale * slope)
    block_weight = jnp.stack([weight_first, -weight_first], axis=1) / length_f
    coeff = (block_weight[:, :, None] * valid).reshape(-1, 1)
    dlogits = (coeff * (target - probs)).astype(jnp.bfloat16)
    dnormed = jnp.dot(dlogits, head_full.T, preferred_element_type=jnp.float32)
    gain_term = jnp.sum(dnormed * flat * inverse, axis=0)
    return (loss_part, dlogits, gain_term)


def on_device(
    thinker_rows,
    codec_ids,
    block_lengths,
    chosen_label,
    ref_logratio,
    pair_count,
    proj_weight,
    norm_gain,
    head_weight,
):
    slots = thinker_rows.shape[2]
    frames = thinker_rows.shape[4]
    thinker_width = thinker_rows.shape[5]
    hold = (slots + 1) // 2
    wide_count = lax.axis_size("wide")
    narrow_count = lax.axis_size("narrow")
    flat_rows = thinker_rows.reshape(slots * 2 * frames, thinker_width)
    projected = jnp.dot(
        flat_rows,
        lax.all_gather(proj_weight, "narrow", axis=0, tiled=True),
        preferred_element_type=jnp.float32,
    ).astype(jnp.bfloat16)
    head_full, gain_full = (
        lax.all_gather(head_weight, "narrow", axis=0, tiled=True),
        lax.all_gather(norm_gain, "narrow", axis=0, tiled=True),
    )
    codes = codec_ids[0, 0]
    lengths = block_lengths[0, 0]
    labels = chosen_label[0, 0]
    ratios = ref_logratio[0, 0]
    live_pairs = jnp.arange(slots, dtype=jnp.int32) < pair_count[0, 0]
    normed, flat, inverse, probs, target, valid, partial_value = forward_terms(
        projected, codes, lengths, live_pairs, gain_full, head_full
    )
    loss_part, dlogits, gain_term = backward_terms(
        partial_value,
        lengths,
        labels,
        ratios,
        live_pairs,
        flat,
        inverse,
        probs,
        target,
        valid,
        head_full,
    )
    pair_total = wide_count * narrow_count * hold
    loss_sum = lax.psum(loss_part, ("wide", "narrow"))
    head_term = jnp.dot(normed.T, dlogits, preferred_element_type=jnp.float32)
    head_piece, gain_piece = (
        lax.psum_scatter(
            head_term.astype(jnp.bfloat16), "narrow", scatter_dimension=0, tiled=True
        ).astype(jnp.float32),
        lax.psum_scatter(
            gain_term.astype(jnp.bfloat16), "narrow", scatter_dimension=0, tiled=True
        ).astype(jnp.float32),
    )
    grad_head, grad_gain = (
        lax.psum(head_piece.astype(jnp.bfloat16), "wide").astype(jnp.float32),
        lax.psum(gain_piece.astype(jnp.bfloat16), "wide").astype(jnp.float32),
    )
    return (loss_sum / pair_total, grad_head, grad_gain)


def solution(mesh):
    in_specs = (
        P("wide", "narrow", None, None, None, None),
        P("wide", "narrow", None, None, None),
        P("wide", "narrow", None, None),
        P("wide", "narrow", None),
        P("wide", "narrow", None),
        P("wide", "narrow"),
        P("narrow", None),
        P("narrow"),
        P("narrow", None),
    )
    out_specs = (P(), P("narrow", None), P("narrow"))
    return jax.shard_map(
        on_device, mesh=mesh, in_specs=in_specs, out_specs=out_specs, check_vma=False
    )
```

profile of v0, /device:TPU:0, one launch (start us, length us, event | category | flops | bytes accessed | tf_op | source)
XLA Modules:
  0.0 342.2 jit_solution(11384165403437378958)
XLA Ops:
  7.2 0.0 copy-start
  7.2 0.0 all-gather.4.cloned.1.call-start
  7.2 0.7 all-gather.4.cloned.1.call-update
  7.9 0.0 all-gather.6.cloned.1.call-start
  8.0 0.7 all-gather.6.cloned.1.call-update
  8.7 0.0 reduce-scatter.2.cloned.1.call-start
  8.7 0.7 compare_bitcast_fusion
  9.4 0.1 copy.27
  9.5 0.7 copy.26
  10.2 0.7 reshape.118
  10.9 12.6 %all-gather = bf16[4,1,256]{2,1,0:T(2,128)(2,1)S(1)} all-gather(bf16[1,1,256]{2,1,0:T(2,128)(2,1)S(1)} %reshape.118), channel_id=1, replica_groups=mesh['wide'=8,'narrow'=4] {'narrow'}, dimensions={0}, use_global_device_ids=true | all-gather | bytes 2560 | tf_op jit(solution)/shard_map/all_gather | solution.py:78
  23.5 0.7 eq.29
  24.8 0.8 copy.22
  25.6 67.5 %all-gather.4.cloned.1.call-done = bf16[2048,1024]{1,0:T(8,128)(2,1)} async-done(((bf16[512,1024]{1,0:T(8,128)(2,1)}), bf16[2048,1024]{1,0:T(8,128)(2,1)}) %all-gather.4.cloned.1.call-update) | async-done | bytes 4194320 | tf_op jit(solution)/shard_map/all_gather | solution.py:73
  93.1 0.0 copy-done
  93.1 6.7 %fusion = (f32[768]{0:T(1024)S(1)}, bf16[768,1024]{1,0:T(8,128)(2,1)}) fusion(bf16[768,2048]{1,0:T(8,128)(2,1)S(1)} %bitcast.36, bf16[2048,1024]{1,0:T(8,128)(2,1)} %all-gather.4.cloned.1.call-done), kind=kOutput, calls=%fused_computation.8 | convolution fusion | flops 3224370432 | bytes 8915968 | tf_op jit(solution)/shard_map/dot_general | solution.py:71
  99.8 74.2 %all-gather.6.cloned.1.call-done = bf16[1024,2048]{1,0:T(8,128)(2,1)} async-done(((bf16[256,2048]{1,0:T(8,128)(2,1)}), bf16[1024,2048]{1,0:T(8,128)(2,1)}) %all-gather.6.cloned.1.call-update) | async-done | bytes 4194320 | tf_op jit(solution)/shard_map/all_gather | solution.py:77
  174.0 5.9 %fusion.15 = (f32[768]{0:T(1024)S(1)}, f32[768,2048]{1,0:T(8,128)S(1)}) fusion(bf16[1024,2048]{1,0:T(8,128)(2,1)} %all-gather.6.cloned.1.call-done, bf16[768,1024]{1,0:T(8,128)(2,1)} %get-tuple-element.14, f32[1024]{0:T(1024)S(1)} %bitcast.37, f32[768]{0:T(1024)S(1)} %add_rsqrt_fusion), kind=kOutput, calls=%fused_computation.37 | convolution fusion | flops 3225943296 | bytes 12068864 | tf_op jit(solution)/shard_map/dot_general | solution.py:16
  179.9 0.0 copy-start.1
  179.9 2.0 exponential_reduce_fusion
  181.9 0.7 copy-done.1
  182.6 0.2 select_reduce_fusion.1
  182.8 0.2 fusion.13
  183.0 0.1 maximum_divide_fusion
  183.0 0.1 fusion.8
  183.1 0.0 copy-start.6
  183.1 4.4 %multiply_convert_fusion = bf16[768,2048]{1,0:T(8,128)(2,1)S(1)} fusion(f32[768,2048]{1,0:T(8,128)} %copy-done.1, f32[768]{0:T(1024)S(1)} %get-tuple-element.10, f32[768]{0:T(1024)S(1)} %mul.90, s32[768]{0:T(1024)S(1)} %eq.29), kind=kLoop, calls=%fused_computation | loop fusion | flops 9437184 | bytes 9446400 | tf_op jit(solution)/shard_map/convert_element_type | solution.py:47
  187.6 0.0 copy-start.2
  187.6 1.7 copy-done.2
  189.2 0.0 copy-done.6
  189.2 5.5 %convolution_convert_fusion = bf16[1024,2048]{1,0:T(8,128)(2,1)} fusion(bf16[768,2048]{1,0:T(8,128)(2,1)S(1)} %multiply_convert_fusion, bf16[768,1024]{1,0:T(8,128)(2,1)S(1)} %copy-done.6, f32[1024]{0:T(1024)S(1)} %bitcast.38, f32[768]{0:T(1024)S(1)} %add_rsqrt_fusion), kind=kOutput, calls=%fused_computation.7 | convolution fusion | flops 3226468352 | bytes 8920064 | tf_op jit(solution)/shard_map/dot_general | solution.py:103
  194.7 0.0 copy-start.5
  194.7 0.0 copy-start.3
  194.7 0.0 copy-start.4
  194.7 0.0 reduce-scatter.2.cloned.1.call-update
  194.7 0.0 all-reduce.3.cloned.1.call-start
  194.8 0.6 copy-done.5
  195.4 0.6 dynamic-slice
  196.0 0.0 copy-done.3
  196.0 0.0 copy-done.4
  196.0 0.6 fusion.12
  197.2 42.8 %psum.21 = f32[]{:T(128)} all-reduce(f32[]{:T(128)} %fusion.12), channel_id=1, replica_groups=mesh['wide'=8,'narrow'=4] {'wide','narrow'}, use_global_device_ids=true, to_apply=%region_6.7 | all-reduce | flops 1 | bytes 8 | tf_op jit(solution)/shard_map/psum | solution.py:102
  240.0 31.2 %reduce-scatter.2.cloned.1.call-done = bf16[256,2048]{1,0:T(8,128)(2,1)} async-done(((bf16[1024,2048]{1,0:T(8,128)(2,1)}), bf16[256,2048]{1,0:T(8,128)(2,1)}) %reduce-scatter.2.cloned.1.call-update) | async-done | bytes 1048592 | tf_op jit(solution)/shard_map/reduce_scatter | solution.py:105
  271.2 0.0 all-reduce.3.cloned.1.call-update
  271.3 7.1 %fusion.4 = bf16[1024]{0:T(1024)(128)(2,1)S(1)} fusion(bf16[768,1024]{1,0:T(8,128)(2,1)} %get-tuple-element.14, bf16[768,2048]{1,0:T(8,128)(2,1)} %copy-done.2, bf16[1024,2048]{1,0:T(8,128)(2,1)} %all-gather.6.cloned.1.call-done, f32[768]{0:T(1024)S(1)} %add_rsqrt_fusion), kind=kOutput, calls=%fused_computation.12 | convolution fusion | flops 3224370176 | bytes 8918016 | tf_op jit(solution)/shard_map/dot_general | solution.py:48
  278.3 10.8 %all-reduce = bf16[1024]{0:T(1024)(128)(2,1)S(1)} all-reduce(bf16[1024]{0:T(1024)(128)(2,1)S(1)} %fusion.4), channel_id=3, replica_groups=mesh['wide'=8,'narrow'=4] {'narrow'}, use_global_device_ids=true, to_apply=%region_10.11.clone | all-reduce | flops 1024 | bytes 4096
  289.2 0.1 dynamic-slice.1
  289.2 12.0 %psum.23 = bf16[256]{0:T(256)(128)(2,1)S(1)} all-reduce(bf16[256]{0:T(256)(128)(2,1)S(1)} %dynamic-slice.1), channel_id=1, replica_groups=mesh['wide'=8,'narrow'=4] {'wide'}, use_global_device_ids=true, to_apply=%region_11.12 | all-reduce | flops 256 | bytes 1024 | tf_op jit(solution)/shard_map/psum | solution.py:114
  301.2 0.6 convert_element_type.53
  302.4 29.3 %all-reduce.3.cloned.1.call-done = bf16[256,2048]{1,0:T(8,128)(2,1)} async-done(((bf16[256,2048]{1,0:T(8,128)(2,1)}), bf16[256,2048]{1,0:T(8,128)(2,1)}) %all-reduce.3.cloned.1.call-update) | async-done | bytes 1048592 | tf_op jit(solution)/shard_map/psum | solution.py:113
  331.7 2.8 convert_element_type.51
  (7 shorter events, 0.1 us)
Async XLA Ops:
  7.2 85.9 %copy-start = (bf16[1,1,3,2,128,2048]{5,4,3,2,1,0:T(8,128)(2,1)S(1)}, bf16[1,1,3,2,128,2048]{5,4,3,2,1,0:T(8,128)(2,1)}, u32[]{:S(2)}) copy-start(bf16[1,1,3,2,128,2048]{5,4,3,2,1,0:T(8,128)(2,1)} %param.9) | copy-start | bytes 9437188
  7.2 85.9 %all-gather.4.cloned.1.call-start = ((), (), s32[]{:S(2)}) async-start(), calls=%async_computation.1 | async-start | bytes 5242880 | tf_op jit(solution)/shard_map/all_gather | solution.py:73
  7.9 166.1 %all-gather.6.cloned.1.call-start = ((), (), s32[]{:S(2)}) async-start(), calls=%async_computation.2 | async-start | bytes 5242880 | tf_op jit(solution)/shard_map/all_gather | solution.py:77
  8.7 262.6 %reduce-scatter.2.cloned.1.call-start = ((), (), s32[]{:S(2)}) async-start(), calls=%async_computation.3 | async-start | bytes 5242880 | tf_op jit(solution)/shard_map/reduce_scatter | solution.py:105
  179.9 2.7 copy-start.1
  183.1 6.1 %copy-start.6 = (bf16[768,1024]{1,0:T(8,128)(2,1)S(1)}, bf16[768,1024]{1,0:T(8,128)(2,1)}, u32[]{:S(2)}) copy-start(bf16[768,1024]{1,0:T(8,128)(2,1)} %get-tuple-element.14) | copy-start | bytes 4718596
  187.6 1.7 copy-start.2
  194.7 0.7 copy-start.5
  194.7 1.3 copy-start.3
  194.7 1.3 copy-start.4
  194.7 137.0 %all-reduce.3.cloned.1.call-start = ((), (), s32[]{:S(2)}) async-start(), calls=%async_computation.4 | async-start | bytes 2097152 | tf_op jit(solution)/shard_map/psum | solution.py:113
Sparse Core Ops, SparseCore 0:
  9.6 83.4 all-gather.3
  94.6 79.2 all-gather.5
  194.9 76.3 reduce-scatter.1
  274.6 57.1 all-reduce.2
where the time goes:
time: 343 us; the launch traced here: 342 us
  waiting for transfers between devices  204 us (59%)
  blocking collectives  78.2 us (23%)
  matrix products  25.2 us (7%)
  between operations  16.9 us (5%)
  other arithmetic  11.5 us (3%)
  local copies, waits for them, and re-layouts  6.64 us (2%)
    all_gather x1, waiting for transfers between devices, on_device(): lax.all_gather(head_weight, 'narrow', axis=0, tiled=True)  74.2 us
    all_gather x1, waiting for transfers between devices, on_device(): lax.all_gather(proj_weight, 'narrow', axis=0, tiled=True)  67.5 us
    psum x1, blocking collectives, on_device(): loss_sum = lax.psum(loss_part, ('wide', 'narrow'))  42.8 us
    reduce_scatter x1, waiting for transfers between devices, on_device(): lax.psum_scatter(head_term.astype(jnp.bfloat16), 'narrow', scatter_dimens...  31.2 us
    psum x1, waiting for transfers between devices, on_device(): lax.psum(head_piece.astype(jnp.bfloat16), 'wide').astype(jnp.float32)  29.3 us
    all_gather x1, blocking collectives, on_device(): lax.all_gather(norm_gain, 'narrow', axis=0, tiled=True)  12.6 us
    psum x1, blocking collectives, on_device(): lax.psum(gain_piece.astype(jnp.bfloat16), 'wide').astype(jnp.float32)  12 us
    unnamed x1, blocking collectives  10.8 us
  transfers between devices with their start and end apart: 4, of which 4 were waited for; matrix products, arithmetic and copies ran while one was open for 6% of the time, Pallas kernels for 0%

commit v1 on v0

v1 whole, which is shorter than its diff:
```python
import functools

import jax
import jax.numpy as jnp
from jax import lax
from jax.experimental import pallas as pl
from jax.experimental.pallas import tpu as pltpu
from jax.sharding import PartitionSpec as P

norm_eps = 1e-06
margin_scale = 2.0
f32 = jnp.float32
bf16 = jnp.bfloat16


def plane_of(wide):
    chips = wide // 2
    rows = 1
    while (rows * 2) * (rows * 2) <= chips:
        rows *= 2
    return rows, chips // rows


def spread_count(nx, ny):
    return 2 * (nx - 1) + 2 * (ny - 1) + 2 * (nx - 1) * (ny - 1) + 1


def copy_count(nx, ny, nz):
    weights = 2 * (nz - 1) * (2 + spread_count(nx, ny)) + (nz - 1)
    sums = nz * (1 + 2 * (nx - 1) + 2 * (ny - 1)) + (nz - 1)
    small = 1 + (nx - 1) + (ny - 1) + (nz - 1)
    return weights + sums + spread_count(nx, ny) + small


def kernel(
    ny, nx, nz, slots, frames, width, dim, vocab, pair_total,
    lengths, labels, counts, ratios,
    rows_in, codes, proj_in, gain_in, head_in,
    loss_out, grad_out, gain_out,
    rows, proj, head, gains, acc, projected, inverse, normed, logits, dlogits,
    term, r1, s1, ra0, ra1, s2a, s2b, rb0, rb1, s3, r3, gather,
    small, sum_c, sum_x, sum_y, sum_z,
    local_sem, send_sem, recv_sem,
):
    w = lax.axis_index("wide")
    z = lax.axis_index("narrow")
    core = lax.rem(w, 2)
    chip = lax.div(w, 2)
    x = lax.rem(chip, nx)
    y = lax.div(chip, nx)
    pair_rows = 2 * frames
    total_rows = slots * pair_rows

    def wide_at(yy, xx, cc):
        return (yy * nx + xx) * 2 + cc

    def shift(i, d, n):
        return lax.rem(i + d, n)

    def x_peer(d):
        return {"wide": wide_at(y, shift(x, d, nx), core), "narrow": z}

    def y_peer(d):
        return {"wide": wide_at(shift(y, d, ny), x, core), "narrow": z}

    def z_peer(d):
        return {"wide": w, "narrow": shift(z, d, nz)}

    mate = {"wide": wide_at(y, x, 1 - core), "narrow": z}
    peers = [mate]
    peers += [x_peer(d) for d in range(1, nx)]
    peers += [y_peer(d) for d in range(1, ny)]
    peers += [z_peer(d) for d in range(1, nz)]

    started = []

    def send(src, dst, device):
        at = len(started)
        copy = pltpu.make_async_remote_copy(
            src_ref=src,
            dst_ref=dst,
            send_sem=send_sem.at[at],
            recv_sem=recv_sem.at[at],
            device_id=device,
            device_id_type=pl.DeviceIdType.MESH,
        )
        copy.start()
        started.append(copy)
        return copy

    def ds(start, size):
        return pl.ds(start if isinstance(start, int) else pl.multiple_of(start, size), size)

    class Tensor:
        def __init__(self, full, shard_rows):
            self.full = full
            self.rows = shard_rows
            self.cols = full.shape[1]
            self.part = shard_rows // 2 // nx
            self.wide = self.cols // 2 // ny

        def box(self, h, xx, yy):
            row = h * (self.rows // 2) + xx * self.part
            return ds(row, self.part), ds((core * ny + yy) * self.wide, self.wide)

        def region(self, zs, h, xx, yy):
            row = zs * self.rows + h * (self.rows // 2) + xx * self.part
            return self.full.at[ds(row, self.part), ds((core * ny + yy) * self.wide, self.wide)]

        def first(self, src, d):
            return [
                send(src.at[self.box(h, x, y)], self.region(z, h, x, y), z_peer(d))
                for h in range(2)
            ]

        def second(self, zs, arrived):
            self.to_x, self.to_y = {}, {}
            out = ({}, {})
            for h in range(2):
                if arrived is not None:
                    arrived[h].wait_recv()
                mine = self.region(zs, h, x, y)
                for d in range(1, nx):
                    out[0][d, h] = send(mine, mine, x_peer(d))
                for d in range(1, ny):
                    out[1][d, h] = send(mine, mine, y_peer(d))
            return out

        def third(self, zs, out):
            later = []
            for d in range(1, nx):
                out[0][d, 0].wait_recv()
                got = self.region(zs, 0, shift(x, nx - d, nx), y)
                later += [send(got, got, y_peer(e)) for e in range(1, ny)]
            for d in range(1, ny):
                out[1][d, 1].wait_recv()
                got = self.region(zs, 1, x, shift(y, ny - d, ny))
                later += [send(got, got, x_peer(e)) for e in range(1, nx)]
            later += [out[0][d, 1] for d in range(1, nx)]
            later += [out[1][d, 0] for d in range(1, ny)]
            return later

        def fourth(self, zs, later):
            for copy in later:
                copy.wait_recv()
            half = self.full.at[ds(zs * self.rows, self.rows), ds(core * (self.cols // 2), self.cols // 2)]
            return send(half, half, mate)

    p_rows, h_rows = width // nz, dim // nz
    proj_t, head_t = Tensor(proj, p_rows), Tensor(head, h_rows)
    out_t = Tensor(gather, h_rows)

    loads = [
        pltpu.make_async_copy(proj_in, proj.at[ds(z * p_rows, p_rows)], local_sem.at[0]),
        pltpu.make_async_copy(rows_in, rows, local_sem.at[1]),
        pltpu.make_async_copy(head_in, head.at[ds(z * h_rows, h_rows)], local_sem.at[2]),
        pltpu.make_async_copy(gain_in, gains.at[z], local_sem.at[3]),
    ]
    for load in loads:
        load.start()
    barrier = pltpu.get_barrier_semaphore()
    for peer in peers:
        pl.semaphore_signal(barrier, inc=1, device_id=peer, device_id_type=pl.DeviceIdType.MESH)
    pl.semaphore_wait(barrier, len(peers))

    order = list(range(1, nz))
    order.sort(key=lambda d: min(d, nz - d))
    items = [(proj_t, d) for d in order] + [(head_t, d) for d in order]
    stage1 = {}
    for d in order:
        stage1[0, d] = proj_t.first(proj_in, d)
    gain_copies = [send(gain_in, gains.at[z], z_peer(d)) for d in order]
    for d in order:
        stage1[1, d] = head_t.first(head_in, d)
    for load in loads:
        load.wait()

    def project(zs, fresh):
        depth = ds(zs * p_rows, p_rows)

        @pl.loop(0, slots)
        def _(p):
            at = ds(p * pair_rows, pair_rows)
            part = jnp.dot(rows[at, depth], proj[depth, :], preferred_element_type=f32)
            acc[at, :] = part if fresh else acc[at, :] + part

    def score(zs, fresh):
        depth = ds(zs * h_rows, h_rows)

        @pl.loop(0, slots)
        def _(p):
            at = ds(p * pair_rows, pair_rows)
            part = jnp.dot(normed[at, depth], head[depth, :], preferred_element_type=f32)
            logits[at, :] = part if fresh else logits[at, :] + part

    def normalise():
        @pl.loop(0, slots * 2)
        def _(b):
            at = ds(b * frames, frames)
            kept = acc[at, :].astype(bf16)
            projected[at, :] = kept
            flat = kept.astype(f32)
            inv = lax.rsqrt(jnp.mean(flat * flat, axis=1, keepdims=True) + norm_eps)
            inverse[at, :] = inv
            for s in range(nz):
                cols = slice(s * h_rows, (s + 1) * h_rows)
                normed[at, cols] = (flat[:, cols] * inv * gains[s, 0:1, :]).astype(bf16)

    stage2, stage3, stage4 = {}, {}, {}
    for t in range(len(items) + 3):
        if t < len(items):
            tensor, d = items[t]
            which = 0 if tensor is proj_t else 1
            stage2[t] = tensor.second(shift(z, nz - d, nz), stage1[which, d])
        if t == 0:
            project(z, True)
        if 0 <= t - 1 < len(items):
            tensor, d = items[t - 1]
            stage3[t - 1] = tensor.third(shift(z, nz - d, nz), stage2[t - 1])
        if 0 <= t - 2 < len(items):
            tensor, d = items[t - 2]
            stage4[t - 2] = tensor.fourth(shift(z, nz - d, nz), stage3[t - 2])
        if 0 <= t - 3 < len(items):
            tensor, d = items[t - 3]
            stage4[t - 3].wait_recv()
            if tensor is proj_t:
                project(shift(z, nz - d, nz), False)
                if t - 3 == nz - 2:
                    for copy in gain_copies:
                        copy.wait_recv()
                    normalise()
                    score(z, True)
            else:
                score(shift(z, nz - d, nz), False)

    small[...] = jnp.zeros_like(small)

    @pl.loop(0, slots)
    def _(p):
        token = lax.broadcasted_iota(jnp.int32, (frames, vocab), 1)
        frame = lax.broadcasted_iota(jnp.int32, (frames, 1), 0)
        scores, sums, valids, sizes = [], [], [], []
        for b in range(2):
            at = ds(p * pair_rows + b * frames, frames)
            values = logits[at, :]
            highest = jnp.max(values, axis=1, keepdims=True)
            powers = jnp.exp(values - highest)
            total = jnp.sum(powers, axis=1, keepdims=True)
            picked = jnp.sum(jnp.where(token == codes[at, :], values, 0.0), axis=1, keepdims=True)
            logits[at, :] = powers
            length = lengths[p, b]
            valid = (frame < length).astype(f32)
            size = jnp.full((1, 1), length.astype(f32), f32)
            logp = picked - (highest + jnp.log(total))
            scores.append(jnp.sum(logp * valid, axis=0, keepdims=True) / size)
            sums.append(total)
            valids.append(valid)
            sizes.append(size)
        sign = jnp.where(labels[p] == 0, 1.0, -1.0).astype(f32)
        live = jnp.where(p < counts[0], 1.0, 0.0).astype(f32)
        margin = margin_scale * (sign * (scores[0] - scores[1]) - ratios[p])
        soft = jnp.maximum(-margin, 0.0) + jnp.log1p(jnp.exp(-jnp.abs(margin)))
        small[:, dim:] += jnp.broadcast_to(soft * live, (small.shape[0], small.shape[1] - dim))
        slope = -jax.nn.sigmoid(-margin) * live
        for b in range(2):
            at = ds(p * pair_rows + b * frames, frames)
            weight = (margin_scale if b == 0 else -margin_scale) * sign * slope / sizes[b]
            coeff = weight * valids[b]
            hot = jnp.where(token == codes[at, :], coeff, 0.0)
            dlogits[at, :] = (hot - (coeff / sums[b]) * logits[at, :]).astype(bf16)

    rx, cy = h_rows // 2 // nx, vocab // 2 // ny
    half_rows, half_cols = h_rows // 2, vocab // 2
    tile = min(512, half_cols)
    moves = list(range(1, nz)) + [0]
    one, two_x, two_y, three_x, three_y, z_copies = {}, {}, {}, {}, {}, {}

    def head_block(k):
        rows_at = ds(shift(z, moves[k], nz) * h_rows, h_rows)

        @pl.loop(0, vocab // tile)
        def _(j):
            cols = ds(j * tile, tile)
            term[k, :, cols] = lax.dot_general(
                normed[:, rows_at], dlogits[:, cols], (((0,), (0,)), ((), ())),
                preferred_element_type=f32,
            ).astype(bf16)

        one[k] = send(term.at[k, :, ds((1 - core) * half_cols, half_cols)], r1.at[k], mate)

    def sum_mates(k):
        one[k].wait_recv()
        mine = term[k, :, ds(core * half_cols, half_cols)].astype(f32)
        s1[k] = (mine + r1[k].astype(f32)).astype(bf16)
        for d in range(1, nx):
            two_x[k, d] = send(s1.at[k, ds(shift(x, d, nx) * rx, rx), :], ra0.at[k, d - 1], x_peer(d))
        for d in range(1, ny):
            two_y[k, d] = send(
                s1.at[k, ds(half_rows, half_rows), ds(shift(y, d, ny) * cy, cy)],
                ra1.at[k, d - 1], y_peer(d),
            )

    def sum_first(k):
        for d in range(1, nx):
            two_x[k, d].wait_recv()
        total = s1[k, ds(x * rx, rx), :].astype(f32)
        for d in range(1, nx):
            total = total + ra0[k, d - 1].astype(f32)
        s2a[k] = total.astype(bf16)
        for d in range(1, ny):
            three_y[k, d] = send(s2a.at[k, :, ds(shift(y, d, ny) * cy, cy)], rb0.at[k, d - 1], y_peer(d))
        for d in range(1, ny):
            two_y[k, d].wait_recv()
        total = s1[k, half_rows:, ds(y * cy, cy)].astype(f32)
        for d in range(1, ny):
            total = total + ra1[k, d - 1].astype(f32)
        s2b[k] = total.astype(bf16)
        for d in range(1, nx):
            three_x[k, d] = send(s2b.at[k, ds(shift(x, d, nx) * rx, rx), :], rb1.at[k, d - 1], x_peer(d))

    def sum_second(k):
        for d in range(1, ny):
            three_y[k, d].wait_recv()
        total = s2a[k, :, ds(y * cy, cy)].astype(f32)
        for d in range(1, ny):
            total = total + rb0[k, d - 1].astype(f32)
        s3[k, :rx, :] = total.astype(bf16)
        for d in range(1, nx):
            three_x[k, d].wait_recv()
        total = s2b[k, ds(x * rx, rx), :].astype(f32)
        for d in range(1, nx):
            total = total + rb1[k, d - 1].astype(f32)
        s3[k, rx:, :] = total.astype(bf16)
        if moves[k]:
            z_copies[moves[k]] = send(s3.at[k], r3.at[moves[k] - 1], z_peer(moves[k]))

    def gain_block(p):
        at = slice(p * pair_rows, (p + 1) * pair_rows)
        dnormed = lax.dot_general(
            dlogits[at, :], head[...], (((1,), (1,)), ((), ())), preferred_element_type=f32
        )
        part = jnp.sum(dnormed * (projected[at, :].astype(f32) * inverse[at, :]), axis=0, keepdims=True)
        small[:, :dim] += jnp.broadcast_to(part, (small.shape[0], dim))

    def share(buffer, value, mine, n, peer):
        buffer[mine] = value
        return [send(buffer.at[mine], buffer.at[mine], peer(d)) for d in range(1, n)]

    def collect(buffer, copies, n):
        for copy in copies:
            copy.wait_recv()
        total = buffer[0]
        for i in range(1, n):
            total = total + buffer[i]
        return total

    small_copies = None
    for t in range(max(nz, slots) + 4):
        if t < nz:
            head_block(t)
        if 0 <= t - 1 < nz:
            sum_mates(t - 1)
        if 0 <= t - 2 < nz:
            sum_first(t - 2)
        if 0 <= t - 3 < nz:
            sum_second(t - 3)
        if 0 <= t - 1 < slots:
            gain_block(t - 1)
        if t == slots:
            small_copies = share(sum_c, small[...], core, 2, lambda d: mate)
        if t == slots + 1:
            value = collect(sum_c, small_copies, 2)
            small_copies = share(sum_x, value, x, nx, x_peer)
        if t == slots + 2:
            value = collect(sum_x, small_copies, nx)
            small_copies = share(sum_y, value, y, ny, y_peer)
        if t == slots + 3:
            value = collect(sum_y, small_copies, ny)
            small_copies = share(sum_z, value, z, nz, z_peer)

    total = s3[nz - 1].astype(f32)
    for d in range(1, nz):
        z_copies[d].wait_recv()
        total = total + r3[d - 1].astype(f32)
    for h in range(2):
        gather[out_t.box(h, x, y)] = total[h * rx : (h + 1) * rx, :].astype(bf16)
    last = out_t.second(0, None)
    value = collect(sum_z, small_copies, nz)
    small[...] = value
    loss_out[...] = value[:, dim:] / pair_total
    gain_out[...] = small[:, ds(z * h_rows, h_rows)]
    last = out_t.fourth(0, out_t.third(0, last))
    mine = ds(core * half_cols, half_cols)
    grad_out[:, mine] = gather[:, mine].astype(f32)
    last.wait_recv()
    other = ds((1 - core) * half_cols, half_cols)
    grad_out[:, other] = gather[:, other].astype(f32)
    for copy in started:
        copy.wait_send()


def on_device(
    thinker_rows, codec_ids, block_lengths, chosen_label, ref_logratio, pair_count,
    proj_weight, norm_gain, head_weight,
):
    slots, frames, width = thinker_rows.shape[2], thinker_rows.shape[4], thinker_rows.shape[5]
    dim, vocab = proj_weight.shape[1], head_weight.shape[1]
    wide, nz = lax.axis_size("wide"), lax.axis_size("narrow")
    ny, nx = plane_of(wide)
    count = slots * 2 * frames
    hold = (slots + 1) // 2
    h_rows = dim // nz
    rx, cy = h_rows // 2 // nx, vocab // 2 // ny
    half = vocab // 2
    n = copy_count(nx, ny, nz)
    vmem, smem = pl.BlockSpec(memory_space=pltpu.VMEM), pl.BlockSpec(memory_space=pltpu.SMEM)
    hbm = pl.BlockSpec(memory_space=pl.ANY)
    line = (8, dim + 128)
    scratch = [
        pltpu.VMEM((count, width), bf16),
        pltpu.VMEM((width, dim), bf16),
        pltpu.VMEM((dim, vocab), bf16),
        pltpu.VMEM((nz, 8, h_rows), f32),
        pltpu.VMEM((count, dim), f32),
        pltpu.VMEM((count, dim), bf16),
        pltpu.VMEM((count, 1), f32),
        pltpu.VMEM((count, dim), bf16),
        pltpu.VMEM((count, vocab), f32),
        pltpu.VMEM((count, vocab), bf16),
        pltpu.VMEM((nz, h_rows, vocab), bf16),
        pltpu.VMEM((nz, h_rows, half), bf16),
        pltpu.VMEM((nz, h_rows, half), bf16),
        pltpu.VMEM((nz, nx - 1, rx, half), bf16),
        pltpu.VMEM((nz, ny - 1, h_rows // 2, cy), bf16),
        pltpu.VMEM((nz, rx, half), bf16),
        pltpu.VMEM((nz, h_rows // 2, cy), bf16),
        pltpu.VMEM((nz, ny - 1, rx, cy), bf16),
        pltpu.VMEM((nz, nx - 1, rx, cy), bf16),
        pltpu.VMEM((nz, 2 * rx, cy), bf16),
        pltpu.VMEM((nz - 1, 2 * rx, cy), bf16),
        pltpu.VMEM((h_rows, vocab), bf16),
        pltpu.VMEM(line, f32),
        pltpu.VMEM((2,) + line, f32),
        pltpu.VMEM((nx,) + line, f32),
        pltpu.VMEM((ny,) + line, f32),
        pltpu.VMEM((nz,) + line, f32),
        pltpu.SemaphoreType.DMA((4,)),
        pltpu.SemaphoreType.DMA((n,)),
        pltpu.SemaphoreType.DMA((n,)),
    ]
    loss, grad_head, grad_gain = pl.pallas_call(
        functools.partial(
            kernel, ny, nx, nz, slots, frames, width, dim, vocab, float(wide * nz * hold)
        ),
        out_shape=[
            jax.ShapeDtypeStruct((8, 128), f32),
            jax.ShapeDtypeStruct((h_rows, vocab), f32),
            jax.ShapeDtypeStruct((8, h_rows), f32),
        ],
        in_specs=[smem, smem, smem, smem, hbm, vmem, hbm, hbm, hbm],
        out_specs=[vmem, vmem, vmem],
        scratch_shapes=scratch,
        compiler_params=pltpu.CompilerParams(
            collective_id=0, has_side_effects=True, vmem_limit_bytes=58 * 1024 * 1024
        ),
        cost_estimate=pl.CostEstimate(
            flops=8 * count * width * dim, bytes_accessed=count * width * 8, transcendentals=count * vocab
        ),
    )(
        block_lengths[0, 0],
        chosen_label[0, 0],
        pair_count[0],
        ref_logratio[0, 0],
        thinker_rows.reshape(count, width),
        codec_ids.reshape(count, 1),
        proj_weight,
        jnp.broadcast_to(norm_gain.astype(f32)[None, :], (8, h_rows)),
        head_weight,
    )
    return loss[0, 0], grad_head, grad_gain[0]


def solution(mesh):
    in_specs = (
        P("wide", "narrow", None, None, None, None),
        P("wide", "narrow", None, None, None),
        P("wide", "narrow", None, None),
        P("wide", "narrow", None),
        P("wide", "narrow", None),
        P("wide", "narrow"),
        P("narrow", None),
        P("narrow"),
        P("narrow", None),
    )
    out_specs = (P(), P("narrow", None), P("narrow"))
    return jax.shard_map(
        on_device, mesh=mesh, in_specs=in_specs, out_specs=out_specs, check_vma=False
    )
```

time: 343 us -> 103 us (0.30)
  waiting for transfers between devices: 204 us -> 0 us
  Pallas kernels: 0 us -> 91.1 us
  blocking collectives: 78.2 us -> 0 us
  matrix products: 25.2 us -> 0 us
  between operations: 16.9 us -> 1.29 us
  other arithmetic: 11.5 us -> 0 us
    all_gather x2 -> x0, waiting for transfers between devices: 142 us -> none  [the longest x1 74.2 us: on_device(): lax.all_gather(head_weight, 'narrow', axis=0, tiled=True)]
    pallas_call x0 -> x1, Pallas kernels: none -> 91.1 us  [on_device(): pl.pallas_call(functools.partial(kernel, ny, nx, nz, slots, frames, width...]
    psum x2 -> x0, blocking collectives: 54.8 us -> none  [the longest x1 42.8 us: on_device(): loss_sum = lax.psum(loss_part, ('wide', 'narrow'))]
    reduce_scatter x1 -> x0, waiting for transfers between devices: 31.2 us -> none  [on_device(): lax.psum_scatter(head_term.astype(jnp.bfloat16), 'narrow', scatter_dimens...]
    psum x1 -> x0, waiting for transfers between devices: 29.3 us -> none  [on_device(): lax.psum(head_piece.astype(jnp.bfloat16), 'wide').astype(jnp.float32)]
    dot_general x4 -> x0, matrix products: 25.2 us -> none  [the longest x1 7.06 us: backward_terms(): dnormed = jnp.dot(dlogits, head_full.T, preferred_element_type=jnp.float32)]
    all_gather x1 -> x0, blocking collectives: 12.6 us -> none  [on_device(): lax.all_gather(norm_gain, 'narrow', axis=0, tiled=True)]
    unnamed x1 -> x0, blocking collectives: 10.8 us -> none
  transfers between devices with their start and end apart: 4 -> 0, of which waited for: 4 -> 0; matrix products, arithmetic and copies ran while one was open for 6% -> 0% of each run, Pallas kernels for 0% -> 0%
where the time goes in v1:
time: 103 us; the launch traced here: 102 us
  Pallas kernels  91.1 us (88%)
  local copies, waits for them, and re-layouts  9.78 us (9%)
  between operations  1.29 us (1%)
    pallas_call x1, Pallas kernels, on_device(): pl.pallas_call(functools.partial(kernel, ny, nx, nz, slots, frames, width...  91.1 us
    unnamed x1, local copies, waits for them, and re-layouts  3.13 us
    slice x2, local copies, waits for them, and re-layouts, on_device(): return (loss[0, 0], grad_head, grad_gain[0])  2.44 us

profile of v1, /device:TPU:0, one launch (start us, length us, event | category | flops | bytes accessed | tf_op | source)
XLA Modules:
  0.0 102.1 jit_solution(12669793816799405176)
XLA Ops:
  1.3 1.3 %copy.13.lengths = s32[3,2]{1,0:T(4,128)} copy(s32[3,2]{0,1:T(2,128)} %bitcast.10) | data formatting | bytes 48 | tf_op jit(solution)/shard_map/squeeze | solution.py:470
  2.6 1.2 %broadcast_in_dim.2.gain_in = f32[8,256]{1,0:T(8,128)} broadcast(bf16[256]{0:T(256)(128)(2,1)} %param.16), dimensions={1} | broadcast | bytes 8704 | tf_op jit(solution)/shard_map/broadcast_in_dim | solution.py:477
  3.9 1.6 %copy.14.codes = s32[768,1]{1,0:T(8,128)} copy(s32[768,1]{0,1:T(1,128)} %bitcast.9) | data formatting | bytes 6144 | tf_op jit(solution)/shard_map/reshape | solution.py:475
  5.5 91.1 %shard_map.112 = (f32[8,128]{1,0:T(8,128)}, f32[256,2048]{1,0:T(8,128)}, f32[8,256]{1,0:T(8,128)}) custom-call(s32[3,2]{1,0:T(4,128)} %copy.13.lengths, s32[3]{0:T(128)} %bitcast.13, s32[1]{0:T(128)} %bitcast.8.counts, f32[3]{0:T(128)} %bitcast.14, bf16[768,2048]{1,0:T(8,128)(2,1)} %bitcast.12, s32[768,1]{1,0:T(8,128)} %copy.14.codes, ...), custom_call_target="tpu_custom_call" | custom-call | flops 12884901888 | bytes 12582912 | tf_op jit(solution)/shard_map/pallas_call | solution.py:451
  96.5 1.2 %slice.6 = f32[1,1]{1,0:T(1,128)} slice(f32[8,128]{1,0:T(8,128)} %get-tuple-element.6), slice={[0:1], [0:1]} | slice | bytes 8 | tf_op jit(solution)/shard_map/slice | solution.py:480
  97.7 1.3 %slice.7 = f32[1,256]{1,0:T(1,128)} slice(f32[8,256]{1,0:T(8,128)} %get-tuple-element.8), slice={[0:1], [0:256]} | slice | bytes 2048 | tf_op jit(solution)/shard_map/slice | solution.py:480
  99.0 3.1 %copy.17 = f32[256,2048]{1,0:T(8,128)} copy(f32[256,2048]{1,0:T(8,128)} %get-tuple-element.13) | data formatting | bytes 4194304

commit v2 on v1

--- a/solution.py
+++ b/solution.py
@@ -26,7 +26,7 @@
 
 
 def copy_count(nx, ny, nz):
-    weights = 2 * (nz - 1) * (2 + spread_count(nx, ny)) + (nz - 1)
+    weights = 2 * (nz - 1) * spread_count(nx, ny) + (nz - 1)
     sums = nz * (1 + 2 * (nx - 1) + 2 * (ny - 1)) + (nz - 1)
     small = 1 + (nx - 1) + (ny - 1) + (nz - 1)
     return weights + sums + spread_count(nx, ny) + small
@@ -34,13 +34,13 @@
 
 def kernel(
     ny, nx, nz, slots, frames, width, dim, vocab, pair_total,
-    lengths, labels, counts, ratios,
-    rows_in, codes, proj_in, gain_in, head_in,
+    labels, counts, ratios, lengths, codes, gain_in,
+    rows_in, proj_in, head_in,
     loss_out, grad_out, gain_out,
-    rows, proj, head, gains, acc, projected, inverse, normed, logits, dlogits,
+    rows, proj, head, gains, acc, projected, inverse, normed, normed_t, logits, dlogits,
     term, r1, s1, ra0, ra1, s2a, s2b, rb0, rb1, s3, r3, gather,
     small, sum_c, sum_x, sum_y, sum_z,
-    local_sem, send_sem, recv_sem,
+    local_sem, send_sem, recv_sem, line_send, line_recv,
 ):
     w = lax.axis_index("wide")
     z = lax.axis_index("narrow")
@@ -107,18 +107,63 @@
             row = zs * self.rows + h * (self.rows // 2) + xx * self.part
             return self.full.at[ds(row, self.part), ds((core * ny + yy) * self.wide, self.wide)]
 
-        def first(self, src, d):
-            return [
-                send(src.at[self.box(h, x, y)], self.region(z, h, x, y), z_peer(d))
-                for h in range(2)
-            ]
-
-        def second(self, zs, arrived):
-            self.to_x, self.to_y = {}, {}
+        def line(self, src, zs, h, send_at, target):
+            which = 0 if self is proj_t else 1
+            here = self.region(zs, h, x, y)
+            return pltpu.make_async_remote_copy(
+                src_ref=here if src is None else src.at[self.box(h, x, y)],
+                dst_ref=here,
+                send_sem=line_send.at[which, h, send_at],
+                recv_sem=line_recv.at[which, h, zs],
+                device_id={"wide": w, "narrow": target},
+                device_id_type=pl.DeviceIdType.MESH,
+            )
+
+        def begin(self, src):
+            for h in range(2):
+                @pl.when(z + 1 < nz)
+                def _():
+                    self.line(src, z, h, z, z + 1).start()
+
+                @pl.when(z > 0)
+                def _():
+                    self.line(src, z, h, nz, z - 1).start()
+
+        def arrive(self, zs, h):
+            self.line(None, zs, h, zs, lax.rem(z + 1, nz)).wait_recv()
+
+            @pl.when((zs < z) & (z + 1 < nz))
+            def _():
+                self.line(None, zs, h, zs, z + 1).start()
+
+            @pl.when((zs > z) & (z > 0))
+            def _():
+                self.line(None, zs, h, zs, z - 1).start()
+
+        def finish(self, src, sources):
+            for h in range(2):
+                @pl.when(z + 1 < nz)
+                def _():
+                    self.line(src, z, h, z, z + 1).wait_send()
+
+                @pl.when(z > 0)
+                def _():
+                    self.line(src, z, h, nz, z - 1).wait_send()
+
+                for zs in sources:
+                    @pl.when((zs < z) & (z + 1 < nz))
+                    def _():
+                        self.line(None, zs, h, zs, z + 1).wait_send()
+
+                    @pl.when((zs > z) & (z > 0))
+                    def _():
+                        self.line(None, zs, h, zs, z - 1).wait_send()
+
+        def second(self, zs, arrives):
             out = ({}, {})
             for h in range(2):
-                if arrived is not None:
-                    arrived[h].wait_recv()
+                if arrives:
+                    self.arrive(zs, h)
                 mine = self.region(zs, h, x, y)
                 for d in range(1, nx):
                     out[0][d, h] = send(mine, mine, x_peer(d))
@@ -154,7 +199,6 @@
         pltpu.make_async_copy(proj_in, proj.at[ds(z * p_rows, p_rows)], local_sem.at[0]),
         pltpu.make_async_copy(rows_in, rows, local_sem.at[1]),
         pltpu.make_async_copy(head_in, head.at[ds(z * h_rows, h_rows)], local_sem.at[2]),
-        pltpu.make_async_copy(gain_in, gains.at[z], local_sem.at[3]),
     ]
     for load in loads:
         load.start()
@@ -163,15 +207,17 @@
         pl.semaphore_signal(barrier, inc=1, device_id=peer, device_id_type=pl.DeviceIdType.MESH)
     pl.semaphore_wait(barrier, len(peers))
 
-    order = list(range(1, nz))
-    order.sort(key=lambda d: min(d, nz - d))
-    items = [(proj_t, d) for d in order] + [(head_t, d) for d in order]
-    stage1 = {}
-    for d in order:
-        stage1[0, d] = proj_t.first(proj_in, d)
-    gain_copies = [send(gain_in, gains.at[z], z_peer(d)) for d in order]
-    for d in order:
-        stage1[1, d] = head_t.first(head_in, d)
+    proj_t.begin(proj_in)
+    gains[z] = jnp.broadcast_to(gain_in[...].astype(f32).reshape(1, h_rows), (8, h_rows))
+    gain_copies = [send(gains.at[z], gains.at[z], z_peer(d)) for d in range(1, nz)]
+    near = jnp.minimum(z, nz - 1 - z)
+    sources = []
+    for j in range(nz - 1):
+        both = j < 2 * near
+        dist = jnp.where(both, j // 2 + 1, j - near + 1)
+        down = jnp.where(both, j % 2 == 0, z > nz - 1 - z)
+        sources.append(jnp.where(down, z - dist, z + dist))
+    items = [(proj_t, zs) for zs in sources] + [(head_t, zs) for zs in sources]
     for load in loads:
         load.wait()
 
@@ -204,34 +250,36 @@
             inverse[at, :] = inv
             for s in range(nz):
                 cols = slice(s * h_rows, (s + 1) * h_rows)
-                normed[at, cols] = (flat[:, cols] * inv * gains[s, 0:1, :]).astype(bf16)
+                part = flat[:, cols] * inv * gains[s, 0:1, :]
+                normed[at, cols] = part.astype(bf16)
+                normed_t[cols, at] = jnp.transpose(part).astype(bf16)
 
     stage2, stage3, stage4 = {}, {}, {}
     for t in range(len(items) + 3):
         if t < len(items):
-            tensor, d = items[t]
-            which = 0 if tensor is proj_t else 1
-            stage2[t] = tensor.second(shift(z, nz - d, nz), stage1[which, d])
+            tensor, zs = items[t]
+            stage2[t] = tensor.second(zs, True)
         if t == 0:
+            head_t.begin(head_in)
             project(z, True)
         if 0 <= t - 1 < len(items):
-            tensor, d = items[t - 1]
-            stage3[t - 1] = tensor.third(shift(z, nz - d, nz), stage2[t - 1])
+            tensor, zs = items[t - 1]
+            stage3[t - 1] = tensor.third(zs, stage2[t - 1])
         if 0 <= t - 2 < len(items):
-            tensor, d = items[t - 2]
-            stage4[t - 2] = tensor.fourth(shift(z, nz - d, nz), stage3[t - 2])
+            tensor, zs = items[t - 2]
+            stage4[t - 2] = tensor.fourth(zs, stage3[t - 2])
         if 0 <= t - 3 < len(items):
-            tensor, d = items[t - 3]
+            tensor, zs = items[t - 3]
             stage4[t - 3].wait_recv()
             if tensor is proj_t:
-                project(shift(z, nz - d, nz), False)
+                project(zs, False)
                 if t - 3 == nz - 2:
                     for copy in gain_copies:
                         copy.wait_recv()
                     normalise()
                     score(z, True)
             else:
-                score(shift(z, nz - d, nz), False)
+                score(zs, False)
 
     small[...] = jnp.zeros_like(small)
 
@@ -239,21 +287,25 @@
     def _(p):
         token = lax.broadcasted_iota(jnp.int32, (frames, vocab), 1)
         frame = lax.broadcasted_iota(jnp.int32, (frames, 1), 0)
-        scores, sums, valids, sizes = [], [], [], []
+        scores, sums, valids, sizes, columns = [], [], [], [], []
         for b in range(2):
             at = ds(p * pair_rows + b * frames, frames)
             values = logits[at, :]
             highest = jnp.max(values, axis=1, keepdims=True)
             powers = jnp.exp(values - highest)
             total = jnp.sum(powers, axis=1, keepdims=True)
-            picked = jnp.sum(jnp.where(token == codes[at, :], values, 0.0), axis=1, keepdims=True)
+            line = codes[0, 0, p, b : b + 1, :].astype(f32)
+            column = jnp.transpose(jnp.broadcast_to(line, (frames, frames)))[:, 0:1].astype(jnp.int32)
+            picked = jnp.sum(jnp.where(token == column, values, 0.0), axis=1, keepdims=True)
             logits[at, :] = powers
-            length = lengths[p, b]
-            valid = (frame < length).astype(f32)
-            size = jnp.full((1, 1), length.astype(f32), f32)
+            held = lengths[0, 0, b : b + 1, :].astype(f32)
+            slot = lax.broadcasted_iota(jnp.int32, (1, slots), 1)
+            size = jnp.sum(jnp.where(slot == p, held, 0.0), axis=1, keepdims=True)
+            valid = (frame.astype(f32) < size).astype(f32)
             logp = picked - (highest + jnp.log(total))
             scores.append(jnp.sum(logp * valid, axis=0, keepdims=True) / size)
             sums.append(total)
+            columns.append(column)
             valids.append(valid)
             sizes.append(size)
         sign = jnp.where(labels[p] == 0, 1.0, -1.0).astype(f32)
@@ -266,7 +318,7 @@
             at = ds(p * pair_rows + b * frames, frames)
             weight = (margin_scale if b == 0 else -margin_scale) * sign * slope / sizes[b]
             coeff = weight * valids[b]
-            hot = jnp.where(token == codes[at, :], coeff, 0.0)
+            hot = jnp.where(token == columns[b], coeff, 0.0)
             dlogits[at, :] = (hot - (coeff / sums[b]) * logits[at, :]).astype(bf16)
 
     rx, cy = h_rows // 2 // nx, vocab // 2 // ny
@@ -281,9 +333,8 @@
         @pl.loop(0, vocab // tile)
         def _(j):
             cols = ds(j * tile, tile)
-            term[k, :, cols] = lax.dot_general(
-                normed[:, rows_at], dlogits[:, cols], (((0,), (0,)), ((), ())),
-                preferred_element_type=f32,
+            term[k, :, cols] = jnp.dot(
+                normed_t[rows_at, :], dlogits[:, cols], preferred_element_type=f32
             ).astype(bf16)
 
         one[k] = send(term.at[k, :, ds((1 - core) * half_cols, half_cols)], r1.at[k], mate)
@@ -355,7 +406,7 @@
         return total
 
     small_copies = None
-    for t in range(max(nz, slots) + 4):
+    for t in range(max(nz, slots) + 3):
         if t < nz:
             head_block(t)
         if 0 <= t - 1 < nz:
@@ -374,9 +425,6 @@
         if t == slots + 2:
             value = collect(sum_x, small_copies, nx)
             small_copies = share(sum_y, value, y, ny, y_peer)
-        if t == slots + 3:
-            value = collect(sum_y, small_copies, ny)
-            small_copies = share(sum_z, value, z, nz, z_peer)
 
     total = s3[nz - 1].astype(f32)
     for d in range(1, nz):
@@ -384,19 +432,27 @@
         total = total + r3[d - 1].astype(f32)
     for h in range(2):
         gather[out_t.box(h, x, y)] = total[h * rx : (h + 1) * rx, :].astype(bf16)
-    last = out_t.second(0, None)
+    last = out_t.second(0, False)
+    value = collect(sum_y, small_copies, ny)
+    small_copies = share(sum_z, value, z, nz, z_peer)
+    last = out_t.fourth(0, out_t.third(0, last))
+    mine = ds(core * half_cols, half_cols)
+    stores = [pltpu.make_async_copy(gather.at[:, mine], grad_out.at[:, mine], local_sem.at[0])]
+    stores[0].start()
     value = collect(sum_z, small_copies, nz)
     small[...] = value
-    loss_out[...] = value[:, dim:] / pair_total
-    gain_out[...] = small[:, ds(z * h_rows, h_rows)]
-    last = out_t.fourth(0, out_t.third(0, last))
-    mine = ds(core * half_cols, half_cols)
-    grad_out[:, mine] = gather[:, mine].astype(f32)
+    loss_out[...] = value[0:1, dim : dim + 1] / pair_total
+    gain_out[...] = small[0:1, ds(z * h_rows, h_rows)]
     last.wait_recv()
     other = ds((1 - core) * half_cols, half_cols)
-    grad_out[:, other] = gather[:, other].astype(f32)
+    stores.append(pltpu.make_async_copy(gather.at[:, other], grad_out.at[:, other], local_sem.at[1]))
+    stores[1].start()
+    for store in stores:
+        store.wait()
     for copy in started:
         copy.wait_send()
+    proj_t.finish(proj_in, sources)
+    head_t.finish(head_in, sources)
 
 
 def on_device(
@@ -425,6 +481,7 @@
         pltpu.VMEM((count, dim), bf16),
         pltpu.VMEM((count, 1), f32),
         pltpu.VMEM((count, dim), bf16),
+        pltpu.VMEM((dim, count), bf16),
         pltpu.VMEM((count, vocab), f32),
         pltpu.VMEM((count, vocab), bf16),
         pltpu.VMEM((nz, h_rows, vocab), bf16),
@@ -447,18 +504,20 @@
         pltpu.SemaphoreType.DMA((4,)),
         pltpu.SemaphoreType.DMA((n,)),
         pltpu.SemaphoreType.DMA((n,)),
+        pltpu.SemaphoreType.DMA((2, 2, nz + 1)),
+        pltpu.SemaphoreType.DMA((2, 2, nz)),
     ]
     loss, grad_head, grad_gain = pl.pallas_call(
         functools.partial(
             kernel, ny, nx, nz, slots, frames, width, dim, vocab, float(wide * nz * hold)
         ),
         out_shape=[
-            jax.ShapeDtypeStruct((8, 128), f32),
-            jax.ShapeDtypeStruct((h_rows, vocab), f32),
-            jax.ShapeDtypeStruct((8, h_rows), f32),
+            jax.ShapeDtypeStruct((1, 1), f32),
+            jax.ShapeDtypeStruct((h_rows, vocab), bf16),
+            jax.ShapeDtypeStruct((1, h_rows), f32),
         ],
-        in_specs=[smem, smem, smem, smem, hbm, vmem, hbm, hbm, hbm],
-        out_specs=[vmem, vmem, vmem],
+        in_specs=[smem, smem, smem, vmem, vmem, vmem, hbm, hbm, hbm],
+        out_specs=[vmem, hbm, vmem],
         scratch_shapes=scratch,
         compiler_params=pltpu.CompilerParams(
             collective_id=0, has_side_effects=True, vmem_limit_bytes=58 * 1024 * 1024
@@ -467,17 +526,17 @@
             flops=8 * count * width * dim, bytes_accessed=count * width * 8, transcendentals=count * vocab
         ),
     )(
-        block_lengths[0, 0],
         chosen_label[0, 0],
         pair_count[0],
         ref_logratio[0, 0],
+        jnp.swapaxes(block_lengths, 2, 3),
+        codec_ids,
+        norm_gain,
         thinker_rows.reshape(count, width),
-        codec_ids.reshape(count, 1),
         proj_weight,
-        jnp.broadcast_to(norm_gain.astype(f32)[None, :], (8, h_rows)),
         head_weight,
     )
-    return loss[0, 0], grad_head, grad_gain[0]
+    return loss[0, 0], grad_head.astype(f32), grad_gain[0]
 
 
 def solution(mesh):

time: 103 us -> 95.6 us (0.928)
  local copies, waits for them, and re-layouts: 9.78 us -> 0.57 us
  Pallas kernels: 91.1 us -> 87.9 us
  other arithmetic: 0 us -> 2.79 us
  between operations: 1.29 us -> 3.07 us
    pallas_call x1, Pallas kernels: 91.1 us -> 87.9 us  [on_device(): pl.pallas_call(functools.partial(kernel, ny, nx, nz, slots, frames, width...]
    convert_element_type x0 -> x1, other arithmetic: none -> 2.79 us  [on_device(): return (loss[0, 0], grad_head.astype(f32), grad_gain[0])]
    unnamed x1 -> x3, local copies, waits for them, and re-layouts: 3.13 us -> 0.57 us
    slice x2 -> x0, local copies, waits for them, and re-layouts: 2.44 us -> none  [on_device(): return (loss[0, 0], grad_head, grad_gain[0])]
    reshape x1 -> x0, local copies, waits for them, and re-layouts: 1.62 us -> none  [on_device(): codec_ids.reshape(count, 1)]
    squeeze x1 -> x0, local copies, waits for them, and re-layouts: 1.34 us -> none  [on_device(): block_lengths[0, 0]]
    broadcast_in_dim x1 -> x0, local copies, waits for them, and re-layouts: 1.25 us -> none  [on_device(): jnp.broadcast_to(norm_gain.astype(f32)[None, :], (8, h_rows))]
where the time goes in v2:
time: 95.6 us; the launch traced here: 94.3 us
  Pallas kernels  87.9 us (92%)
  between operations  3.07 us (3%)
  other arithmetic  2.79 us (3%)
    pallas_call x1, Pallas kernels, on_device(): pl.pallas_call(functools.partial(kernel, ny, nx, nz, slots, frames, width...  87.9 us
    convert_element_type x1, other arithmetic, on_device(): return (loss[0, 0], grad_head.astype(f32), grad_gain[0])  2.79 us

profile of v2, /device:TPU:0, one launch (start us, length us, event | category | flops | bytes accessed | tf_op | source)
XLA Modules:
  0.0 94.3 jit_solution(13849708361280478738)
XLA Ops:
  1.3 87.9 %shard_map.112 = (f32[1,1]{1,0:T(1,128)}, bf16[256,2048]{1,0:T(8,128)(2,1)}, f32[1,256]{1,0:T(1,128)}) custom-call(s32[3]{0:T(128)} %bitcast.11, s32[1]{0:T(128)} %bitcast.7.counts, f32[3]{0:T(128)} %bitcast.12, s32[1,1,2,3]{3,2,1,0:T(2,128)} %bitcast.10, s32[1,1,3,2,128]{4,3,2,1,0:T(2,128)} %codes.1, bf16[256]{0:T(256)(128)(2,1)} %gain_in.1, ...), custom_call_target="tpu_custom_call" | custom-call | flops 12884901888 | bytes 12582912 | tf_op jit(solution)/shard_map/pallas_call | solution.py:510
  89.2 0.0 copy-start
  89.2 2.8 %convert_element_type.3 = f32[256,2048]{1,0:T(8,128)} convert(bf16[256,2048]{1,0:T(8,128)(2,1)} %get-tuple-element.7) | non-fusion elementwise | flops 524288 | bytes 3145728 | tf_op jit(solution)/shard_map/convert_element_type | solution.py:539
  92.6 0.0 copy-done
  92.7 0.6 copy.16
Async XLA Ops:
  89.2 3.4 %copy-start = (f32[1,256]{1,0:T(1,128)S(1)}, f32[1,256]{1,0:T(1,128)}, u32[]{:S(2)}) copy-start(f32[1,256]{1,0:T(1,128)} %get-tuple-element.8) | copy-start | bytes 3076

commit v3 on v2

--- a/solution.py
+++ b/solution.py
@@ -9,6 +9,7 @@
 
 norm_eps = 1e-06
 margin_scale = 2.0
+halves = 2
 f32 = jnp.float32
 bf16 = jnp.bfloat16
 
@@ -26,10 +27,10 @@
 
 
 def copy_count(nx, ny, nz):
-    weights = 2 * (nz - 1) * spread_count(nx, ny) + (nz - 1)
-    sums = nz * (1 + 2 * (nx - 1) + 2 * (ny - 1)) + (nz - 1)
-    small = 1 + (nx - 1) + (ny - 1) + (nz - 1)
-    return weights + sums + spread_count(nx, ny) + small
+    weights = 3 * (nz - 1) * spread_count(nx, ny) + (nz - 1)
+    sums = halves * (nz * (1 + 2 * (nx - 1) + 2 * (ny - 1)) + (nz - 1))
+    small = (nz - 1) + (2 * nx * ny - 1)
+    return weights + sums + halves * spread_count(nx, ny) + small
 
 
 def kernel(
@@ -39,7 +40,7 @@
     loss_out, grad_out, gain_out,
     rows, proj, head, gains, acc, projected, inverse, normed, normed_t, logits, dlogits,
     term, r1, s1, ra0, ra1, s2a, s2b, rb0, rb1, s3, r3, gather,
-    small, sum_c, sum_x, sum_y, sum_z,
+    small, sum_z, sum_w,
     local_sem, send_sem, recv_sem, line_send, line_recv,
 ):
     w = lax.axis_index("wide")
@@ -66,10 +67,13 @@
     def z_peer(d):
         return {"wide": w, "narrow": shift(z, d, nz)}
 
+    wide = ny * nx * 2
     mate = {"wide": wide_at(y, x, 1 - core), "narrow": z}
-    peers = [mate]
-    peers += [x_peer(d) for d in range(1, nx)]
-    peers += [y_peer(d) for d in range(1, ny)]
+
+    def w_peer(d):
+        return {"wide": shift(w, d, wide), "narrow": z}
+
+    peers = [w_peer(d) for d in range(1, wide)]
     peers += [z_peer(d) for d in range(1, nz)]
 
     started = []
@@ -92,23 +96,27 @@
         return pl.ds(start if isinstance(start, int) else pl.multiple_of(start, size), size)
 
     class Tensor:
-        def __init__(self, full, shard_rows):
+        def __init__(self, full, shard_rows, base, cols, index):
             self.full = full
             self.rows = shard_rows
-            self.cols = full.shape[1]
+            self.base = base
+            self.cols = cols
+            self.index = index
             self.part = shard_rows // 2 // nx
-            self.wide = self.cols // 2 // ny
+            self.wide = cols // 2 // ny
+
+        def columns(self, yy):
+            return ds(self.base + (core * ny + yy) * self.wide, self.wide)
 
         def box(self, h, xx, yy):
-            row = h * (self.rows // 2) + xx * self.part
-            return ds(row, self.part), ds((core * ny + yy) * self.wide, self.wide)
+            return ds(h * (self.rows // 2) + xx * self.part, self.part), self.columns(yy)
 
         def region(self, zs, h, xx, yy):
             row = zs * self.rows + h * (self.rows // 2) + xx * self.part
-            return self.full.at[ds(row, self.part), ds((core * ny + yy) * self.wide, self.wide)]
+            return self.full.at[ds(row, self.part), self.columns(yy)]
 
         def line(self, src, zs, h, send_at, target):
-            which = 0 if self is proj_t else 1
+            which = self.index
             here = self.region(zs, h, x, y)
             return pltpu.make_async_remote_copy(
                 src_ref=here if src is None else src.at[self.box(h, x, y)],
@@ -188,12 +196,14 @@
         def fourth(self, zs, later):
             for copy in later:
                 copy.wait_recv()
-            half = self.full.at[ds(zs * self.rows, self.rows), ds(core * (self.cols // 2), self.cols // 2)]
+            half = self.full.at[ds(zs * self.rows, self.rows), ds(self.base + core * (self.cols // 2), self.cols // 2)]
             return send(half, half, mate)
 
     p_rows, h_rows = width // nz, dim // nz
-    proj_t, head_t = Tensor(proj, p_rows), Tensor(head, h_rows)
-    out_t = Tensor(gather, h_rows)
+    piece = vocab // halves
+    proj_t = Tensor(proj, p_rows, 0, dim, 0)
+    head_t = [Tensor(head, h_rows, q * piece, piece, 1 + q) for q in range(halves)]
+    out_t = [Tensor(gather, h_rows, q * piece, piece, 0) for q in range(halves)]
 
     loads = [
         pltpu.make_async_copy(proj_in, proj.at[ds(z * p_rows, p_rows)], local_sem.at[0]),
@@ -217,7 +227,7 @@
         dist = jnp.where(both, j // 2 + 1, j - near + 1)
         down = jnp.where(both, j % 2 == 0, z > nz - 1 - z)
         sources.append(jnp.where(down, z - dist, z + dist))
-    items = [(proj_t, zs) for zs in sources] + [(head_t, zs) for zs in sources]
+    items = [(proj_t, zs) for zs in sources] + [(head_t[q], zs) for zs in sources for q in range(halves)]
     for load in loads:
         load.wait()
 
@@ -230,14 +240,15 @@
             part = jnp.dot(rows[at, depth], proj[depth, :], preferred_element_type=f32)
             acc[at, :] = part if fresh else acc[at, :] + part
 
-    def score(zs, fresh):
+    def score(zs, q, fresh):
         depth = ds(zs * h_rows, h_rows)
+        cols = slice(q * piece, (q + 1) * piece)
 
         @pl.loop(0, slots)
         def _(p):
             at = ds(p * pair_rows, pair_rows)
-            part = jnp.dot(normed[at, depth], head[depth, :], preferred_element_type=f32)
-            logits[at, :] = part if fresh else logits[at, :] + part
+            part = jnp.dot(normed[at, depth], head[depth, cols], preferred_element_type=f32)
+            logits[at, cols] = part if fresh else logits[at, cols] + part
 
     def normalise():
         @pl.loop(0, slots * 2)
@@ -260,7 +271,8 @@
             tensor, zs = items[t]
             stage2[t] = tensor.second(zs, True)
         if t == 0:
-            head_t.begin(head_in)
+            for half in head_t:
+                half.begin(head_in)
             project(z, True)
         if 0 <= t - 1 < len(items):
             tensor, zs = items[t - 1]
@@ -277,9 +289,10 @@
                     for copy in gain_copies:
                         copy.wait_recv()
                     normalise()
-                    score(z, True)
             else:
-                score(zs, False)
+                if t - 3 < nz - 1 + halves:
+                    score(z, tensor.index - 1, True)
+                score(zs, tensor.index - 1, False)
 
     small[...] = jnp.zeros_like(small)
 
@@ -321,20 +334,21 @@
             hot = jnp.where(token == columns[b], coeff, 0.0)
             dlogits[at, :] = (hot - (coeff / sums[b]) * logits[at, :]).astype(bf16)
 
-    rx, cy = h_rows // 2 // nx, vocab // 2 // ny
-    half_rows, half_cols = h_rows // 2, vocab // 2
+    rx, cy = h_rows // 2 // nx, piece // 2 // ny
+    half_rows, half_cols = h_rows // 2, piece // 2
     tile = min(512, half_cols)
-    moves = list(range(1, nz)) + [0]
+    moves = [(d, q) for d in list(range(1, nz)) + [0] for q in range(halves)]
+    blocks = len(moves)
     one, two_x, two_y, three_x, three_y, z_copies = {}, {}, {}, {}, {}, {}
 
     def head_block(k):
-        rows_at = ds(shift(z, moves[k], nz) * h_rows, h_rows)
-
-        @pl.loop(0, vocab // tile)
+        rows_at = ds(shift(z, moves[k][0], nz) * h_rows, h_rows)
+        base = moves[k][1] * piece
+
+        @pl.loop(0, piece // tile)
         def _(j):
-            cols = ds(j * tile, tile)
-            term[k, :, cols] = jnp.dot(
-                normed_t[rows_at, :], dlogits[:, cols], preferred_element_type=f32
+            term[k, :, ds(j * tile, tile)] = jnp.dot(
+                normed_t[rows_at, :], dlogits[:, ds(base + j * tile, tile)], preferred_element_type=f32
             ).astype(bf16)
 
         one[k] = send(term.at[k, :, ds((1 - core) * half_cols, half_cols)], r1.at[k], mate)
@@ -382,16 +396,25 @@
         for d in range(1, nx):
             total = total + rb1[k, d - 1].astype(f32)
         s3[k, rx:, :] = total.astype(bf16)
-        if moves[k]:
-            z_copies[moves[k]] = send(s3.at[k], r3.at[moves[k] - 1], z_peer(moves[k]))
+        d, q = moves[k]
+        if d:
+            z_copies[d, q] = send(s3.at[k], r3.at[(d - 1) * halves + q], z_peer(d))
 
     def gain_block(p):
-        at = slice(p * pair_rows, (p + 1) * pair_rows)
+        at = slice(p * frames, (p + 1) * frames)
         dnormed = lax.dot_general(
             dlogits[at, :], head[...], (((1,), (1,)), ((), ())), preferred_element_type=f32
         )
         part = jnp.sum(dnormed * (projected[at, :].astype(f32) * inverse[at, :]), axis=0, keepdims=True)
         small[:, :dim] += jnp.broadcast_to(part, (small.shape[0], dim))
+
+    def finish_block(q):
+        total = s3[blocks - halves + q].astype(f32)
+        for d in range(1, nz):
+            z_copies[d, q].wait_recv()
+            total = total + r3[(d - 1) * halves + q].astype(f32)
+        for h in range(2):
+            gather[out_t[q].box(h, x, y)] = total[h * rx : (h + 1) * rx, :].astype(bf16)
 
     def share(buffer, value, mine, n, peer):
         buffer[mine] = value
@@ -405,54 +428,57 @@
             total = total + buffer[i]
         return total
 
+    last2, last3, last4 = {}, {}, {}
     small_copies = None
-    for t in range(max(nz, slots) + 3):
-        if t < nz:
+    for t in range(blocks + 5):
+        if t < blocks:
             head_block(t)
-        if 0 <= t - 1 < nz:
+        if 0 <= t - 1 < blocks:
             sum_mates(t - 1)
-        if 0 <= t - 2 < nz:
+        if 0 <= t - 2 < blocks:
             sum_first(t - 2)
-        if 0 <= t - 3 < nz:
+        if 0 <= t - 3 < blocks:
             sum_second(t - 3)
-        if 0 <= t - 1 < slots:
-            gain_block(t - 1)
-        if t == slots:
-            small_copies = share(sum_c, small[...], core, 2, lambda d: mate)
-        if t == slots + 1:
-            value = collect(sum_c, small_copies, 2)
-            small_copies = share(sum_x, value, x, nx, x_peer)
-        if t == slots + 2:
-            value = collect(sum_x, small_copies, nx)
-            small_copies = share(sum_y, value, y, ny, y_peer)
-
-    total = s3[nz - 1].astype(f32)
-    for d in range(1, nz):
-        z_copies[d].wait_recv()
-        total = total + r3[d - 1].astype(f32)
-    for h in range(2):
-        gather[out_t.box(h, x, y)] = total[h * rx : (h + 1) * rx, :].astype(bf16)
-    last = out_t.second(0, False)
-    value = collect(sum_y, small_copies, ny)
-    small_copies = share(sum_z, value, z, nz, z_peer)
-    last = out_t.fourth(0, out_t.third(0, last))
-    mine = ds(core * half_cols, half_cols)
-    stores = [pltpu.make_async_copy(gather.at[:, mine], grad_out.at[:, mine], local_sem.at[0])]
-    stores[0].start()
-    value = collect(sum_z, small_copies, nz)
+        q = t - 3 - (blocks - halves)
+        if 0 <= q < halves:
+            finish_block(q)
+            last2[q] = out_t[q].second(0, False)
+        if 0 <= q - 1 < halves:
+            last3[q - 1] = out_t[q - 1].third(0, last2[q - 1])
+        if 0 <= q - 2 < halves:
+            last4[q - 2] = out_t[q - 2].fourth(0, last3[q - 2])
+        if 0 <= t - 2 < min(slots * 2, blocks - 1):
+            gain_block(t - 2)
+        if t == blocks:
+            for p in range(blocks - 1, slots * 2):
+                gain_block(p)
+            small_copies = share(sum_z, small[...], z, nz, z_peer)
+        if t == blocks + 2:
+            value = collect(sum_z, small_copies, nz)
+            small_copies = share(sum_w, value, w, wide, w_peer)
+    stores = []
+    for q in range(halves):
+        mine = ds(q * piece + core * half_cols, half_cols)
+        stores.append(pltpu.make_async_copy(gather.at[:, mine], grad_out.at[:, mine], local_sem.at[q]))
+        stores[q].start()
+    value = collect(sum_w, small_copies, wide)
     small[...] = value
     loss_out[...] = value[0:1, dim : dim + 1] / pair_total
     gain_out[...] = small[0:1, ds(z * h_rows, h_rows)]
-    last.wait_recv()
-    other = ds((1 - core) * half_cols, half_cols)
-    stores.append(pltpu.make_async_copy(gather.at[:, other], grad_out.at[:, other], local_sem.at[1]))
-    stores[1].start()
+    for q in range(halves):
+        last4[q].wait_recv()
+        other = ds(q * piece + (1 - core) * half_cols, half_cols)
+        stores.append(
+            pltpu.make_async_copy(gather.at[:, other], grad_out.at[:, other], local_sem.at[halves + q])
+        )
+        stores[halves + q].start()
     for store in stores:
         store.wait()
     for copy in started:
         copy.wait_send()
     proj_t.finish(proj_in, sources)
-    head_t.finish(head_in, sources)
+    for half in head_t:
+        half.finish(head_in, sources)
 
 
 def on_device(
@@ -466,8 +492,10 @@
     count = slots * 2 * frames
     hold = (slots + 1) // 2
     h_rows = dim // nz
-    rx, cy = h_rows // 2 // nx, vocab // 2 // ny
-    half = vocab // 2
+    piece = vocab // halves
+    rx, cy = h_rows // 2 // nx, piece // 2 // ny
+    half = piece // 2
+    nb = nz * halves
     n = copy_count(nx, ny, nz)
     vmem, smem = pl.BlockSpec(memory_space=pltpu.VMEM), pl.BlockSpec(memory_space=pltpu.SMEM)
     hbm = pl.BlockSpec(memory_space=pl.ANY)
@@ -484,28 +512,26 @@
         pltpu.VMEM((dim, count), bf16),
         pltpu.VMEM((count, vocab), f32),
         pltpu.VMEM((count, vocab), bf16),
-        pltpu.VMEM((nz, h_rows, vocab), bf16),
-        pltpu.VMEM((nz, h_rows, half), bf16),
-        pltpu.VMEM((nz, h_rows, half), bf16),
-        pltpu.VMEM((nz, nx - 1, rx, half), bf16),
-        pltpu.VMEM((nz, ny - 1, h_rows // 2, cy), bf16),
-        pltpu.VMEM((nz, rx, half), bf16),
-        pltpu.VMEM((nz, h_rows // 2, cy), bf16),
-        pltpu.VMEM((nz, ny - 1, rx, cy), bf16),
-        pltpu.VMEM((nz, nx - 1, rx, cy), bf16),
-        pltpu.VMEM((nz, 2 * rx, cy), bf16),
-        pltpu.VMEM((nz - 1, 2 * rx, cy), bf16),
+        pltpu.VMEM((nb, h_rows, piece), bf16),
+        pltpu.VMEM((nb, h_rows, half), bf16),
+        pltpu.VMEM((nb, h_rows, half), bf16),
+        pltpu.VMEM((nb, nx - 1, rx, half), bf16),
+        pltpu.VMEM((nb, ny - 1, h_rows // 2, cy), bf16),
+        pltpu.VMEM((nb, rx, half), bf16),
+        pltpu.VMEM((nb, h_rows // 2, cy), bf16),
+        pltpu.VMEM((nb, ny - 1, rx, cy), bf16),
+        pltpu.VMEM((nb, nx - 1, rx, cy), bf16),
+        pltpu.VMEM((nb, 2 * rx, cy), bf16),
+        pltpu.VMEM((nb - halves, 2 * rx, cy), bf16),
         pltpu.VMEM((h_rows, vocab), bf16),
         pltpu.VMEM(line, f32),
-        pltpu.VMEM((2,) + line, f32),
-        pltpu.VMEM((nx,) + line, f32),
-        pltpu.VMEM((ny,) + line, f32),
         pltpu.VMEM((nz,) + line, f32),
+        pltpu.VMEM((wide,) + line, f32),
         pltpu.SemaphoreType.DMA((4,)),
         pltpu.SemaphoreType.DMA((n,)),
         pltpu.SemaphoreType.DMA((n,)),
-        pltpu.SemaphoreType.DMA((2, 2, nz + 1)),
-        pltpu.SemaphoreType.DMA((2, 2, nz)),
+        pltpu.SemaphoreType.DMA((1 + halves, 2, nz + 1)),
+        pltpu.SemaphoreType.DMA((1 + halves, 2, nz)),
     ]
     loss, grad_head, grad_gain = pl.pallas_call(
         functools.partial(

time: 95.6 us -> 105 us (1.098)
  Pallas kernels: 87.9 us -> 97.3 us
    pallas_call x1, Pallas kernels: 87.9 us -> 97.3 us  [on_device(): pl.pallas_call(functools.partial(kernel, ny, nx, nz, slots, frames, width...]
where the time goes in v3:
time: 105 us; the launch traced here: 104 us
  Pallas kernels  97.3 us (93%)
  between operations  3.07 us (3%)
  other arithmetic  2.79 us (3%)
    pallas_call x1, Pallas kernels, on_device(): pl.pallas_call(functools.partial(kernel, ny, nx, nz, slots, frames, width...  97.3 us
    convert_element_type x1, other arithmetic, on_device(): return (loss[0, 0], grad_head.astype(f32), grad_gain[0])  2.79 us

profile of v3, /device:TPU:0, one launch (start us, length us, event | category | flops | bytes accessed | tf_op | source)
XLA Modules:
  0.0 103.7 jit_solution(13728133476220470522)
XLA Ops:
  1.3 97.3 %shard_map.112 = (f32[1,1]{1,0:T(1,128)}, bf16[256,2048]{1,0:T(8,128)(2,1)}, f32[1,256]{1,0:T(1,128)}) custom-call(s32[3]{0:T(128)} %bitcast.11, s32[1]{0:T(128)} %bitcast.7.counts, f32[3]{0:T(128)} %bitcast.12, s32[1,1,2,3]{3,2,1,0:T(2,128)} %bitcast.10, s32[1,1,3,2,128]{4,3,2,1,0:T(2,128)} %codes.1, bf16[256]{0:T(256)(128)(2,1)} %gain_in.1, ...), custom_call_target="tpu_custom_call" | custom-call | flops 12884901888 | bytes 12582912 | tf_op jit(solution)/shard_map/pallas_call | solution.py:536
  98.6 0.0 copy-start
  98.6 2.8 %convert_element_type.3 = f32[256,2048]{1,0:T(8,128)} convert(bf16[256,2048]{1,0:T(8,128)(2,1)} %get-tuple-element.7) | non-fusion elementwise | flops 524288 | bytes 3145728 | tf_op jit(solution)/shard_map/convert_element_type | solution.py:565
  102.0 0.0 copy-done
  102.0 0.6 copy.16
Async XLA Ops:
  98.6 3.4 %copy-start = (f32[1,256]{1,0:T(1,128)S(1)}, f32[1,256]{1,0:T(1,128)}, u32[]{:S(2)}) copy-start(f32[1,256]{1,0:T(1,128)} %get-tuple-element.8) | copy-start | bytes 3076
